TPU v7x, 256 devices: a whole 4x4x8 slice. The times are simulated.
256 devices in a mesh: dp: 16 (over y_lo, z), ctx: 16 (over x, y_hi, core).
Axes of the slice: x: 4, y: 4 (y_hi: 2, y_lo: 2; y = y_hi * 2 + y_lo), z: 8, core: 2. Of those that a mesh axis runs over, the one named last changes fastest.
Arguments:
- queries: bfloat16 [16, 2048, 4096], P('dp', 'ctx'), may hold values from -9 to 9
- keys: bfloat16 [16, 2048, 512], P('dp', 'ctx'), may hold values from -7 to 7
- values: bfloat16 [16, 2048, 512], P('dp', 'ctx'), may hold values from -6 to 6
- cotangent: bfloat16 [16, 2048, 4096], P('dp', 'ctx'), may hold values from -6 to 6
- live: int32 [16, 2048], P('dp', 'ctx'), may hold values from 0 to 1, as said below
- docs: int32 [16, 2048], P('dp'), may hold values from 0 to 5, never falling along the last dimension, each value on 1 to 1024 neighbouring positions
Outputs:
- attended: bfloat16 [16, 2048, 4096], P('dp', 'ctx')
- grad_queries: bfloat16 [16, 2048, 4096], P('dp', 'ctx')
- key_gradient: bfloat16 [16, 2048, 512], P('dp', 'ctx')
- value_gradient: bfloat16 [16, 2048, 512], P('dp', 'ctx')
Inputs may be any that keep to these rules, and one draw needn't show every extreme that they name: `docs`: never falls along a sequence; each document spans 1 to 1024 positions and one spans exactly 1024. `live`: row 0 of every sequence is 1.
All inputs are finite; a program needn't handle non-finite values.
Results may differ from a plain program's by a relative error of at most 0.02.
Values may be sent and summed in bfloat16 or wider, within the bound.
No kernel may reach another device: no remote copies, remote signals or barrier semaphores. Data moves between devices by JAX's collectives and lax.ppermute only.
A program may use at most 64 MiB of HBM per device.

v0:
```python
from functools import partial
import math

import jax
import jax.numpy as jnp
from jax import lax
from jax.experimental import pallas as pl
from jax.experimental.pallas import tpu as pltpu
from jax.sharding import PartitionSpec as P

HEAD = 128
BLOCK = 128
TILE = 256
GROUPS = 2
FOLD = 8
ROWS = FOLD * BLOCK
MASKED = -1e30
SCALE = 1.0 / math.sqrt(HEAD)
SCALE_LOG2E = SCALE * math.log2(math.e)

TERM_ROWS = 2 * GROUPS * HEAD + 16
DIGIT = 32

NT = (((1,), (1,)), ((), ()))
NN = (((1,), (0,)), ((), ()))


def dot(a, b, dims=NN):
    return lax.dot_general(a, b, dims, preferred_element_type=jnp.float32)


def attention_kernel(
    me_ref,
    count_ref,
    docs_ref,
    live_own,
    live_sib,
    q_own,
    q_sib,
    c_own,
    c_sib,
    *refs,
):
    chips = 8
    chunks = refs[:chips]
    o_own, dq_own, sib_out = refs[chips : chips + 3]
    terms = refs[chips + 3 : 2 * chips + 3]
    (
        k_nat,
        v_nat,
        s_ref,
        p_ref,
        q_ref,
        do_ref,
        qt_ref,
        dot_ref,
        m_ref,
        o_ref,
        dq_ref,
        dkt_ref,
        dvt_ref,
    ) = refs[2 * chips + 3 :]

    me = me_ref[0]
    core, chip = me & 1, me >> 1
    line, side = chip >> 1, chip & 1
    lows = []
    for step in (0, 1, 3, 2):
        for other in range(2):
            lows.append(2 * ((line + step) & 3) + (side ^ other))

    for group in range(GROUPS):
        k_nat[group, 0:BLOCK, :] = jnp.zeros((BLOCK, HEAD), jnp.bfloat16)
        v_nat[group, 0:BLOCK, :HEAD] = jnp.zeros((BLOCK, HEAD), jnp.bfloat16)
        v_nat[group, :, HEAD:] = jnp.ones((v_nat.shape[1], HEAD), jnp.bfloat16)
    for at, chunk in enumerate(chunks):
        low = lows[at]
        for half in range(2):
            block = low if half == 0 else 15 - low
            place = pl.ds(pl.multiple_of((block + 1) * BLOCK, BLOCK), BLOCK)
            rows = slice(half * BLOCK, (half + 1) * BLOCK)
            for group in range(GROUPS):
                k_nat[group, place, :] = chunk[rows, group * HEAD : (group + 1) * HEAD]
                v_nat[group, place, :HEAD] = chunk[
                    rows, (GROUPS + group) * HEAD : (GROUPS + group + 1) * HEAD
                ]

    count = jnp.sum(count_ref[...].astype(jnp.float32), axis=1, keepdims=True)
    upper = jnp.floor(count * (1.0 / (DIGIT * DIGIT)))
    rest = count - upper * (DIGIT * DIGIT)
    middle = jnp.floor(rest * (1.0 / DIGIT))
    digit_row = lax.broadcasted_iota(jnp.int32, (16, 2 * BLOCK), 0)
    digits = jnp.where(digit_row == 0, rest - middle * DIGIT, 0.0)
    digits = jnp.where(digit_row == 1, middle, jnp.where(digit_row == 2, upper, digits))
    digits = digits.astype(jnp.bfloat16)

    def column(row):
        return jnp.broadcast_to(row.astype(jnp.float32), (BLOCK, BLOCK)).T[:, :1]

    all_docs = docs_ref[...].astype(jnp.float32)
    live_columns = column(live_own[...]), column(live_sib[...])
    bounds = []
    for half in range(2):
        block = chip if half == 0 else 15 - chip
        swapped = core if half == 0 else 1 - core
        own_docs = column(docs_ref[:, pl.ds(pl.multiple_of(block * BLOCK, BLOCK), BLOCK)])
        own_docs = jnp.where(
            swapped == 1, jnp.concatenate([own_docs[64:], own_docs[:64]], axis=0), own_docs
        )
        below = jnp.where(all_docs < own_docs, 1.0, 0.0)
        low_bound = jnp.sum(below, axis=1, keepdims=True)
        tiles = (block * BLOCK + BLOCK - jnp.min(low_bound).astype(jnp.int32) + TILE - 1) >> 8
        row = lax.broadcasted_iota(jnp.int32, (BLOCK, 1), 0)
        own_pos = block * BLOCK + ((row + 64 * swapped) & (BLOCK - 1))
        live = jnp.concatenate(
            [col[half * 64 : half * 64 + 64] for col in live_columns], axis=0
        )
        bounds.append((tiles, low_bound.astype(jnp.int32), own_pos, live))

    for group in range(GROUPS):
        dkt_ref[...] = jnp.zeros_like(dkt_ref)
        dvt_ref[...] = jnp.zeros_like(dvt_ref)
        for half in range(2):
            tiles, low_bound, own_pos, live = bounds[half]
            end = ((chip if half == 0 else 15 - chip) + 1) * BLOCK
            rows = slice(half * 64, half * 64 + 64)
            dq_rows = slice(BLOCK + half * 64, BLOCK + half * 64 + 64)

            def columns(head):
                return slice((group * FOLD + head) * HEAD, (group * FOLD + head + 1) * HEAD)

            def from_columns(head):
                start = core * (GROUPS * FOLD * HEAD) + (group * FOLD + head) * HEAD
                return pl.ds(pl.multiple_of(start, HEAD), HEAD)

            for head in range(FOLD):
                q_ref[head * BLOCK : head * BLOCK + 64, :] = q_own[rows, from_columns(head)]
                q_ref[head * BLOCK + 64 : (head + 1) * BLOCK, :] = q_sib[rows, from_columns(head)]

            def key_rows(j):
                return pl.ds(pl.multiple_of(end - TILE * (j + 1) + BLOCK, BLOCK), TILE)

            def tile_columns(j):
                return pl.ds(pl.multiple_of(j * TILE, TILE), TILE)

            def over_tiles(body):
                body(0, True)

                @pl.loop(1, tiles)
                def _(j):
                    body(j, False)

            def score_tile(j, first_tile):
                first = end - TILE * (j + 1)
                key_pos = first + lax.broadcasted_iota(jnp.int32, (BLOCK, TILE), 1)
                bias = jnp.where((key_pos >= low_bound) & (key_pos <= own_pos), 0.0, MASKED)
                scores = dot(q_ref[...], k_nat[group, key_rows(j), :], NT)
                scores = (
                    scores.reshape(FOLD, BLOCK, TILE) * SCALE_LOG2E + bias[None]
                ).reshape(ROWS, TILE)
                s_ref[:, tile_columns(j)] = scores
                peak = jnp.maximum(scores[:, :HEAD], scores[:, HEAD:])
                m_ref[...] = peak if first_tile else jnp.maximum(m_ref[...], peak)

            over_tiles(score_tile)
            m_ref[...] = jnp.broadcast_to(
                jnp.max(m_ref[...], axis=1, keepdims=True), (ROWS, HEAD)
            )

            def weight_tile(j, first_tile):
                peak = m_ref[...]
                scores = s_ref[:, tile_columns(j)]
                left = jnp.exp2(scores[:, :HEAD] - peak)
                right = jnp.exp2(scores[:, HEAD:] - peak)
                weights = jnp.concatenate([left, right], axis=1).astype(jnp.bfloat16)
                p_ref[:, tile_columns(j)] = weights
                part = dot(weights, v_nat[group, key_rows(j), :])
                o_ref[...] = part if first_tile else o_ref[...] + part

            over_tiles(weight_tile)
            for head in range(FOLD):
                span = slice(head * BLOCK, (head + 1) * BLOCK)
                inverse = 1.0 / o_ref[span, HEAD:]
                out = (o_ref[span, :HEAD] * inverse).astype(jnp.bfloat16)
                o_own[rows, columns(head)] = out[:64]
                sib_out[rows, columns(head)] = out[64:]
                cot = jnp.concatenate(
                    [c_own[rows, from_columns(head)], c_sib[rows, from_columns(head)]], axis=0
                )
                grad = (cot.astype(jnp.float32) * (live * inverse)).astype(jnp.bfloat16)
                do_ref[span, :] = grad
                m_ref[span, :] = jnp.broadcast_to(
                    jnp.sum(
                        grad.astype(jnp.float32) * out.astype(jnp.float32), axis=1, keepdims=True
                    ),
                    (BLOCK, HEAD),
                )
            qt_ref[...] = q_ref[...].T
            dot_ref[...] = do_ref[...].T

            def gradient_tile(j, first_tile):
                delta = m_ref[...]
                pushes = dot(do_ref[...], v_nat[group, key_rows(j), :HEAD], NT)
                weights = p_ref[:, tile_columns(j)]
                wide = weights.astype(jnp.float32)
                slopes = jnp.concatenate(
                    [
                        wide[:, :HEAD] * (pushes[:, :HEAD] - delta),
                        wide[:, HEAD:] * (pushes[:, HEAD:] - delta),
                    ],
                    axis=1,
                ).astype(jnp.bfloat16)
                part = dot(slopes, k_nat[group, key_rows(j), :])
                dq_ref[...] = part if first_tile else dq_ref[...] + part
                dkt_ref[:, key_rows(j)] += dot(qt_ref[...], slopes)
                dvt_ref[:, key_rows(j)] += dot(dot_ref[...], weights)

            over_tiles(gradient_tile)
            for head in range(FOLD):
                span = slice(head * BLOCK, (head + 1) * BLOCK)
                out = (dq_ref[span, :] * SCALE).astype(jnp.bfloat16)
                dq_own[rows, columns(head)] = out[:64]
                sib_out[dq_rows, columns(head)] = out[64:]
        for at, term in enumerate(terms):
            low = lows[at]
            if group == 0:
                term[2 * GROUPS * HEAD :, :] = digits
            for half in range(2):
                block = low if half == 0 else 15 - low
                place = pl.ds(pl.multiple_of((block + 1) * BLOCK, BLOCK), BLOCK)
                lanes = slice(half * BLOCK, (half + 1) * BLOCK)
                term[group * HEAD : (group + 1) * HEAD, lanes] = (
                    dkt_ref[:, place] * SCALE
                ).astype(jnp.bfloat16)
                term[(GROUPS + group) * HEAD : (GROUPS + group + 1) * HEAD, lanes] = dvt_ref[
                    :, place
                ].astype(jnp.bfloat16)


def attention(me, count, docs, live_own, live_sib, q_own, q_sib, c_own, c_sib, chunks, interpret=False):
    vmem = pl.BlockSpec(memory_space=pltpu.VMEM)
    half_rows = jax.ShapeDtypeStruct((128, GROUPS * FOLD * HEAD), jnp.bfloat16)
    both_rows = jax.ShapeDtypeStruct((256, GROUPS * FOLD * HEAD), jnp.bfloat16)
    term = jax.ShapeDtypeStruct((TERM_ROWS, 2 * BLOCK), jnp.bfloat16)
    padded = 2048 + BLOCK
    most = 5
    return pl.pallas_call(
        attention_kernel,
        out_shape=(half_rows, half_rows, both_rows) + (term,) * 8,
        in_specs=[pl.BlockSpec(memory_space=pltpu.SMEM)] + [vmem] * 16,
        out_specs=(vmem,) * 11,
        scratch_shapes=[
            pltpu.VMEM((GROUPS, padded, HEAD), jnp.bfloat16),
            pltpu.VMEM((GROUPS, padded, 2 * HEAD), jnp.bfloat16),
            pltpu.VMEM((ROWS, most * TILE), jnp.float32),
            pltpu.VMEM((ROWS, most * TILE), jnp.bfloat16),
            pltpu.VMEM((ROWS, HEAD), jnp.bfloat16),
            pltpu.VMEM((ROWS, HEAD), jnp.bfloat16),
            pltpu.VMEM((HEAD, ROWS), jnp.bfloat16),
            pltpu.VMEM((HEAD, ROWS), jnp.bfloat16),
            pltpu.VMEM((ROWS, HEAD), jnp.float32),
            pltpu.VMEM((ROWS, 2 * HEAD), jnp.float32),
            pltpu.VMEM((ROWS, HEAD), jnp.float32),
            pltpu.VMEM((HEAD, padded), jnp.float32),
            pltpu.VMEM((HEAD, padded), jnp.float32),
        ],
        compiler_params=pltpu.CompilerParams(vmem_limit_bytes=28 * 1024 * 1024),
        cost_estimate=pl.CostEstimate(
            flops=6_000_000_000, bytes_accessed=8_000_000, transcendentals=4_000_000
        ),
        interpret=interpret,
    )(me, count, docs, live_own, live_sib, q_own, q_sib, c_own, c_sib, *chunks)


def closing_kernel(me_ref, *refs):
    terms, (kept, sent, ratio) = refs[:4], refs[4:]
    total = sum(term[...].astype(jnp.float32) for term in terms)
    width = 2 * GROUPS * HEAD
    digits = total[width : width + 8, :HEAD]
    count = digits[0:1] + DIGIT * (digits[1:2] + DIGIT * digits[2:3])
    ratio_row = 32768.0 / count
    ratio[...] = jnp.broadcast_to(ratio_row, (8, HEAD))
    rows = (total[:width] * ratio_row[:, :1]).T
    outer = jnp.concatenate([rows[:64], rows[192:]], axis=0).astype(jnp.bfloat16)
    inner = rows[64:192].astype(jnp.bfloat16)
    first = (me_ref[0] & 1) == 0
    kept[...] = jnp.where(first, outer, inner)
    sent[...] = jnp.where(first, inner, outer)


def closing(me, terms):
    vmem = pl.BlockSpec(memory_space=pltpu.VMEM)
    rows = jax.ShapeDtypeStruct((BLOCK, 2 * GROUPS * HEAD), jnp.bfloat16)
    return pl.pallas_call(
        closing_kernel,
        out_shape=(rows, rows, jax.ShapeDtypeStruct((8, HEAD), jnp.float32)),
        in_specs=[pl.BlockSpec(memory_space=pltpu.SMEM)] + [vmem] * 4,
        out_specs=(vmem,) * 3,
        compiler_params=pltpu.CompilerParams(vmem_limit_bytes=8 * 1024 * 1024),
        cost_estimate=pl.CostEstimate(flops=1_000_000, bytes_accessed=1_000_000, transcendentals=0),
    )(me, *terms)


def scale_kernel(me_ref, ratio, own, got, out):
    at = pl.program_id(0)
    mine = (at >> 1) == (me_ref[0] & 1)
    columns = pl.ds(pl.multiple_of((at & 1) * 1024, 1024), 1024)
    factor = ratio[0:1, 0:1]

    @pl.when(mine)
    def _():
        out[...] = (own[:, columns].astype(jnp.float32) * factor).astype(jnp.bfloat16)

    @pl.when(jnp.logical_not(mine))
    def _():
        out[...] = (got[BLOCK:, columns].astype(jnp.float32) * factor).astype(jnp.bfloat16)


def scaled(me, ratio, own, got):
    vmem = pl.BlockSpec(memory_space=pltpu.VMEM)
    return pl.pallas_call(
        scale_kernel,
        grid=(4,),
        out_shape=jax.ShapeDtypeStruct((BLOCK, 4096), jnp.bfloat16),
        in_specs=[pl.BlockSpec(memory_space=pltpu.SMEM)] + [vmem] * 3,
        out_specs=pl.BlockSpec((BLOCK, 1024), lambda i: (0, i)),
        compiler_params=pltpu.CompilerParams(vmem_limit_bytes=8 * 1024 * 1024),
        cost_estimate=pl.CostEstimate(flops=1_000_000, bytes_accessed=2_000_000, transcendentals=0),
    )(me, ratio, own, got)


def join_kernel(me_ref, kept, got, keys, values):
    first = (me_ref[0] & 1) == 0
    width = GROUPS * HEAD
    for at, out in enumerate((keys, values)):
        columns = slice(at * width, (at + 1) * width)
        own, other = kept[:, columns], got[:, columns]
        out[:, :width] = jnp.where(first, own, other)
        out[:, width:] = jnp.where(first, other, own)


def joined(me, kept, got):
    vmem = pl.BlockSpec(memory_space=pltpu.VMEM)
    whole = pl.BlockSpec((BLOCK, 2 * GROUPS * HEAD), lambda i: (0, 0))
    rows = jax.ShapeDtypeStruct((BLOCK, 2 * GROUPS * HEAD), jnp.bfloat16)
    return pl.pallas_call(
        join_kernel,
        grid=(1,),
        out_shape=(rows, rows),
        in_specs=[pl.BlockSpec(memory_space=pltpu.SMEM)] + [vmem] * 2,
        out_specs=(whole, whole),
        compiler_params=pltpu.CompilerParams(vmem_limit_bytes=4 * 1024 * 1024),
        cost_estimate=pl.CostEstimate(flops=100_000, bytes_accessed=500_000, transcendentals=0),
    )(me, kept, got)


def on_device(queries, keys, values, cotangent, live, docs):
    me = lax.axis_index("ctx")
    core = me % 2

    def move(shift):
        return [(i, (i + shift) % 16) for i in range(16)]

    def swap(bit):
        return [(i, i ^ bit) for i in range(16)]

    def to_right(a):
        return lax.ppermute(a, "ctx", move(4))

    def to_left(a):
        return lax.ppermute(a, "ctx", move(-4))

    def to_side(a):
        return lax.ppermute(a, "ctx", swap(2))

    def to_core(a):
        return lax.ppermute(a, "ctx", swap(1))

    kv_width = GROUPS * HEAD
    q_width = GROUPS * FOLD * HEAD
    keys_got, values_got = to_core(keys[0]), to_core(values[0])
    q_got, c_got = to_core(queries[0]), to_core(cotangent[0])

    def groups(a, b):
        chosen = [jnp.where(core == 0, x[:, :kv_width], x[:, kv_width:]) for x in (a, b)]
        return jnp.concatenate(chosen, axis=1)

    kv_keep, kv_got = groups(keys[0], values[0]), groups(keys_got, values_got)
    first = jnp.where(core == 0, kv_keep, kv_got)
    second = jnp.where(core == 0, kv_got, kv_keep)
    mine = jnp.concatenate([first[:64], second[:64], second[64:], first[64:]], axis=0)

    live_got = to_core(live)
    count = live + live_got
    for bit in (1, 2):
        count = count + lax.ppermute(count, "dp", swap(bit))
    count, _ = lax.optimization_barrier((count, mine))
    count = count + lax.ppermute(count, "dp", swap(4))

    from_left = to_right(mine)
    from_right = to_left(mine)
    beside = to_side(mine)
    beside, from_left, from_right, count = lax.optimization_barrier(
        (beside, from_left, from_right, count)
    )
    beside_left = to_right(beside)
    beside_right = to_left(beside)
    opposite = to_right(from_left)
    beside_opposite = to_left(beside_right)
    count, _, _ = lax.optimization_barrier((count, beside_left, beside_right))
    count = count + lax.ppermute(count, "dp", swap(8))
    chunks = (
        mine,
        beside,
        from_right,
        beside_right,
        from_left,
        beside_left,
        opposite,
        beside_opposite,
    )

    device = me.reshape(1).astype(jnp.int32)
    results = attention(
        device,
        count,
        docs,
        live,
        live_got,
        queries[0],
        q_got,
        cotangent[0],
        c_got,
        chunks,
    )
    o_own, dq_own, sib_out = results[:3]
    sib_got = to_core(sib_out)
    t_mine, t_beside, t_right, t_beside_right, t_left, t_beside_left, t_opp, t_beside_opp = (
        results[3:]
    )

    def add(*terms):
        return sum(t.astype(jnp.float32) for t in terms).astype(jnp.bfloat16)

    opp_via_right = to_right(t_opp)
    opp_via_left = to_left(t_beside_opp)
    got_beside_1 = to_right(t_beside_right)
    right_sum, left_sum = add(t_right, opp_via_right), add(t_beside_left, opp_via_left)
    got_mine_2 = to_right(right_sum)
    got_beside_2 = to_left(left_sum)
    got_mine_1 = to_left(t_left)
    beside_sum = add(t_beside, got_beside_1, got_beside_2)
    got_side = to_side(beside_sum)
    def join(own, got, width):
        low = jnp.where(core == 0, own, got)
        high = jnp.where(core == 0, got, own)
        return jnp.concatenate([low, high], axis=1)

    attended = join(o_own, sib_got[:BLOCK], q_width)[None]
    t_mine, attended = lax.optimization_barrier((t_mine, attended))
    kept, sent, ratio = closing(device, (t_mine, got_mine_1, got_mine_2, got_side))
    got = to_core(sent)

    grad_queries = scaled(device, ratio, dq_own, sib_got)[None]
    got, grad_queries = lax.optimization_barrier((got, grad_queries))
    key_gradient, value_gradient = joined(device, kept, got)
    return attended, grad_queries, key_gradient[None], value_gradient[None]


def solution(mesh):
    rows = P("dp", "ctx", None)
    return jax.shard_map(
        on_device,
        mesh=mesh,
        in_specs=(rows, rows, rows, rows, P("dp", "ctx"), P("dp", None)),
        out_specs=(rows, rows, rows, rows),
        check_vma=False,
    )
```

profile of v0, /device:TPU:31, one launch (start us, length us, event | category | flops | bytes accessed | tf_op | source)
XLA Modules:
  0.0 102.3 jit_solution(2545929492817881980)
XLA Ops:
  0.6 0.8 collective-permute-start.5
  2.0 0.4 collective-permute-start.13
  2.4 0.7 add.32
  3.1 1.6 %collective-permute-start.6 = (s32[1,128]{1,0:T(1,128)S(1)}, s32[1,128]{1,0:T(1,128)S(1)}, u32[]{:S(2)}, u32[]{:S(2)}) collective-permute-start(s32[1,128]{1,0:T(1,128)S(1)} %add.32), channel_id=1, source_target_pairs={{0,16},{16,0},{32,48},{48,32},{64,80},{80,64},{96,112},{112,96},{1... | collective-permute-start | bytes 1544 | tf_op jit(solution)/shard_map/ppermute | solution.py:396
  4.7 0.9 collective-permute-done.6
  5.7 3.1 %collective-permute-start.7 = (s32[1,128]{1,0:T(1,128)S(1)}, s32[1,128]{1,0:T(1,128)S(1)}, u32[]{:S(2)}, u32[]{:S(2)}) collective-permute-start(s32[1,128]{1,0:T(1,128)S(1)} %add.33), channel_id=1, source_target_pairs={{0,32},{16,48},{32,0},{48,16},{64,96},{80,112},{96,64},{112,80},{1... | collective-permute-start | bytes 1544 | tf_op jit(solution)/shard_map/ppermute | solution.py:396
  8.7 1.0 slice_select_fusion.2
  9.9 6.1 %collective-permute-start.8 = (s32[1,128]{1,0:T(1,128)S(1)}, s32[1,128]{1,0:T(1,128)S(1)}, u32[]{:S(2)}, u32[]{:S(2)}) collective-permute-start(s32[1,128]{1,0:T(1,128)S(1)} %add.34), channel_id=1, source_target_pairs={{0,64},{16,80},{32,96},{48,112},{64,0},{80,16},{96,32},{112,48},{1... | collective-permute-start | bytes 1544 | tf_op jit(solution)/shard_map/ppermute | solution.py:398
  16.0 0.5 collective-permute-start.4
  16.6 2.1 %collective-permute-start.3 = (bf16[256,512]{1,0:T(8,128)(2,1)S(1)}, bf16[256,512]{1,0:T(8,128)(2,1)S(1)}, u32[]{:S(2)}, u32[]{:S(2)}) collective-permute-start(bf16[256,512]{1,0:T(8,128)(2,1)S(1)} %pad_maximum_fusion.refs_0_), channel_id=1, source_target_pairs={{0,4},{1,5},{2,6},{3,7},{4,8},{5,9},{6,10},{7,11},{8,12},{9,13},{1... | collective-permute-start | bytes 786440 | tf_op jit(solution)/shard_map/ppermute | solution.py:368
  18.7 1.0 collective-permute-start.2
  19.7 2.8 %collective-permute-done.4.refs_2_ = bf16[256,512]{1,0:T(8,128)(2,1)S(1)} collective-permute-done((bf16[256,512]{1,0:T(8,128)(2,1)S(1)}, bf16[256,512]{1,0:T(8,128)(2,1)S(1)}, u32[]{:S(2)}, u32[]{:S(2)}) %collective-permute-start.4) | collective-permute-done | bytes 262176 | tf_op jit(solution)/shard_map/ppermute | solution.py:371
  22.5 3.0 %collective-permute-done.2.refs_1_ = bf16[256,512]{1,0:T(8,128)(2,1)S(1)} collective-permute-done((bf16[256,512]{1,0:T(8,128)(2,1)S(1)}, bf16[256,512]{1,0:T(8,128)(2,1)S(1)}, u32[]{:S(2)}, u32[]{:S(2)}) %collective-permute-start.2) | collective-permute-done | bytes 262176 | tf_op jit(solution)/shard_map/ppermute | solution.py:374
  25.4 2.7 %collective-permute-start.9 = (bf16[256,512]{1,0:T(8,128)(2,1)S(1)}, bf16[256,512]{1,0:T(8,128)(2,1)S(1)}, u32[]{:S(2)}, u32[]{:S(2)}) collective-permute-start(bf16[256,512]{1,0:T(8,128)(2,1)S(1)} %collective-permute-done.2.refs_1_), channel_id=1, source_target_pairs={{0,4},{1,5},{2,6},{3,7},{4,8},{5,9},{6,10},{7,11},{8,12},{9,13},{1... | collective-permute-start | bytes 786440 | tf_op jit(solution)/shard_map/ppermute | solution.py:368
  28.1 3.7 %collective-permute-done.10.refs_3_ = bf16[256,512]{1,0:T(8,128)(2,1)S(1)} collective-permute-done((bf16[256,512]{1,0:T(8,128)(2,1)S(1)}, bf16[256,512]{1,0:T(8,128)(2,1)S(1)}, u32[]{:S(2)}, u32[]{:S(2)}) %collective-permute-start.10) | collective-permute-done | bytes 262176 | tf_op jit(solution)/shard_map/ppermute | solution.py:371
  31.9 0.8 collective-permute-start.11
  32.6 1.9 %collective-permute-done.11 = s32[1,128]{1,0:T(1,128)S(1)} collective-permute-done((s32[1,128]{1,0:T(1,128)S(1)}, s32[1,128]{1,0:T(1,128)S(1)}, u32[]{:S(2)}, u32[]{:S(2)}) %collective-permute-start.11) | collective-permute-done | bytes 544 | tf_op jit(solution)/shard_map/ppermute | solution.py:411
  34.6 5.1 %collective-permute-done.15.refs_7_ = bf16[256,512]{1,0:T(8,128)(2,1)S(1)} collective-permute-done((bf16[256,512]{1,0:T(8,128)(2,1)S(1)}, bf16[256,512]{1,0:T(8,128)(2,1)S(1)}, u32[]{:S(2)}, u32[]{:S(2)}) %collective-permute-start.15) | collective-permute-done | bytes 262176 | tf_op jit(solution)/shard_map/ppermute | solution.py:371
  39.7 23.7 %shard_map.93 = (bf16[128,2048]{1,0:T(8,128)(2,1)S(1)}, bf16[128,2048]{1,0:T(8,128)(2,1)S(1)}, bf16[256,2048]{1,0:T(8,128)(2,1)S(1)}, bf16[528,256]{1,0:T(8,128)...) custom-call(s32[1]{0:T(128)} %bitcast.me_ref, ...), custom_call_target="tpu_custom_call" | custom-call | flops 6000000000 | bytes 8000000 | tf_op jit(solution)/shard_map/pallas_call | solution.py:247
  63.4 6.8 %collective-permute-start.16 = (bf16[256,2048]{1,0:T(8,128)(2,1)S(1)}, bf16[256,2048]{1,0:T(8,128)(2,1)S(1)}, u32[]{:S(2)}, u32[]{:S(2)}) collective-permute-start(bf16[256,2048]{1,0:T(8,128)(2,1)S(1)} %get-tuple-element.38), channel_id=1, source_target_pairs={{0,1},{1,0},{2,3},{3,2},{4,5},{5,4},{6,7},{7,6},{8,9},{9,8},{10,11... | collective-permute-start | bytes 3145736 | tf_op jit(solution)/shard_map/ppermute | solution.py:377
  70.3 2.7 %collective-permute-start.18 = (bf16[528,256]{1,0:T(8,128)(2,1)S(1)}, bf16[528,256]{1,0:T(8,128)(2,1)S(1)}, u32[]{:S(2)}, u32[]{:S(2)}) collective-permute-start(bf16[528,256]{1,0:T(8,128)(2,1)S(1)} %get-tuple-element.43), channel_id=1, source_target_pairs={{0,4},{1,5},{2,6},{3,7},{4,8},{5,9},{6,10},{7,11},{8,12},{9,13},{1... | collective-permute-start | bytes 811016 | tf_op jit(solution)/shard_map/ppermute | solution.py:368
  73.0 6.5 %collective-permute-done.21 = bf16[528,256]{1,0:T(8,128)(2,1)S(1)} collective-permute-done((bf16[528,256]{1,0:T(8,128)(2,1)S(1)}, bf16[528,256]{1,0:T(8,128)(2,1)S(1)}, u32[]{:S(2)}, u32[]{:S(2)}) %collective-permute-start.21) | collective-permute-done | bytes 270368 | tf_op jit(solution)/shard_map/ppermute | solution.py:371
  80.1 2.7 %collective-permute-start.19 = (bf16[528,256]{1,0:T(8,128)(2,1)S(1)}, bf16[528,256]{1,0:T(8,128)(2,1)S(1)}, u32[]{:S(2)}, u32[]{:S(2)}) collective-permute-start(bf16[528,256]{1,0:T(8,128)(2,1)S(1)} %add_convert_fusion.2), channel_id=1, source_target_pairs={{0,4},{1,5},{2,6},{3,7},{4,8},{5,9},{6,10},{7,11},{8,12},{9,13},{1... | collective-permute-start | bytes 811016 | tf_op jit(solution)/shard_map/ppermute | solution.py:368
  82.8 1.4 %collective-permute-done.20 = bf16[528,256]{1,0:T(8,128)(2,1)S(1)} collective-permute-done((bf16[528,256]{1,0:T(8,128)(2,1)S(1)}, bf16[528,256]{1,0:T(8,128)(2,1)S(1)}, u32[]{:S(2)}, u32[]{:S(2)}) %collective-permute-start.20) | collective-permute-done | bytes 270368 | tf_op jit(solution)/shard_map/ppermute | solution.py:368
  84.2 4.0 %collective-permute-done.22 = bf16[528,256]{1,0:T(8,128)(2,1)S(1)} collective-permute-done((bf16[528,256]{1,0:T(8,128)(2,1)S(1)}, bf16[528,256]{1,0:T(8,128)(2,1)S(1)}, u32[]{:S(2)}, u32[]{:S(2)}) %collective-permute-start.22) | collective-permute-done | bytes 270368 | tf_op jit(solution)/shard_map/ppermute | solution.py:371
  88.3 0.7 collective-permute-start.23
  89.1 1.1 %maximum_bitcast_fusion = bf16[1,128,4096]{2,1,0:T(8,128)(2,1)} fusion(bf16[128,2048]{1,0:T(8,128)(2,1)S(1)} %get-tuple-element.57, bf16[128,2048]{1,0:T(8,128)(2,1)S(1)} %get-tuple-element.56), kind=kLoop, calls=%fused_computation | loop fusion | flops 2097152 | bytes 2097152 | tf_op jit(solution)/shard_map/broadcast_in_dim | solution.py:459
  90.2 3.8 %collective-permute-done.17.refs_1_ = bf16[528,256]{1,0:T(8,128)(2,1)S(1)} collective-permute-done((bf16[528,256]{1,0:T(8,128)(2,1)S(1)}, bf16[528,256]{1,0:T(8,128)(2,1)S(1)}, u32[]{:S(2)}, u32[]{:S(2)}) %collective-permute-start.17) | collective-permute-done | bytes 270368 | tf_op jit(solution)/shard_map/ppermute | solution.py:371
  94.0 1.2 %collective-permute-done.23.refs_3_ = bf16[528,256]{1,0:T(8,128)(2,1)S(1)} collective-permute-done((bf16[528,256]{1,0:T(8,128)(2,1)S(1)}, bf16[528,256]{1,0:T(8,128)(2,1)S(1)}, u32[]{:S(2)}, u32[]{:S(2)}) %collective-permute-start.23) | collective-permute-done | bytes 270368 | tf_op jit(solution)/shard_map/ppermute | solution.py:374
  95.5 4.4 %collective-permute-start.24 = (bf16[128,512]{1,0:T(8,128)(2,1)S(1)}, bf16[128,512]{1,0:T(8,128)(2,1)S(1)}, u32[]{:S(2)}, u32[]{:S(2)}) collective-permute-start(bf16[128,512]{1,0:T(8,128)(2,1)S(1)} %get-tuple-element.48), channel_id=1, source_target_pairs={{0,1},{1,0},{2,3},{3,2},{4,5},{5,4},{6,7},{7,6},{8,9},{9,8},{10,11... | collective-permute-start | bytes 393224 | tf_op jit(solution)/shard_map/ppermute | solution.py:377
  99.8 1.7 %shard_map.95 = bf16[128,4096]{1,0:T(8,128)(2,1)} custom-call(s32[1]{0:T(128)} %bitcast.me_ref, f32[8,128]{1,0:T(8,128)S(1)} %get-tuple-element.49.ratio, bf16[128,2048]{1,0:T(8,128)(2,1)S(1)} %get-tuple-element.50.own, bf16[256,2048]{1,0:T(8,128)(2,1)S(1)} %collective-permute-done.16.got), custom_call_target="tpu_custom_call" | custom-call | flops 1000000 | bytes 2000000 | tf_op jit(solution)/shard_map/pallas_call | solution.py:321
  101.6 0.7 shard_map.96
  (46 shorter events, 1.8 us)
Async XLA Ops:
  0.6 1.8 %collective-permute-start.5 = (s32[1,128]{1,0:T(1,128)}, s32[1,128]{1,0:T(1,128)S(1)}, u32[]{:S(2)}, u32[]{:S(2)}) collective-permute-start(s32[1,128]{1,0:T(1,128)} %live_own.1), channel_id=1, source_target_pairs={{0,1},{1,0},{2,3},{3,2},{4,5},{5,4},{6,7},{7,6},{8,9},{9,8},{10,11... | collective-permute-start | bytes 1544 | tf_op jit(solution)/shard_map/ppermute | solution.py:377
  1.4 8.3 %collective-permute-start = (bf16[128,512]{1,0:T(8,128)(2,1)}, bf16[128,512]{1,0:T(8,128)(2,1)S(1)}, u32[]{:S(2)}, u32[]{:S(2)}) collective-permute-start(bf16[128,512]{1,0:T(8,128)(2,1)} %bitcast.15), channel_id=1, source_target_pairs={{0,1},{1,0},{2,3},{3,2},{4,5},{5,4},{6,7},{7,6},{8,9},{9,8},{10,11... | collective-permute-start | bytes 393224 | tf_op jit(solution)/shard_map/ppermute | solution.py:377
  1.5 8.3 %collective-permute-start.1 = (bf16[128,512]{1,0:T(8,128)(2,1)}, bf16[128,512]{1,0:T(8,128)(2,1)S(1)}, u32[]{:S(2)}, u32[]{:S(2)}) collective-permute-start(bf16[128,512]{1,0:T(8,128)(2,1)} %bitcast.17), channel_id=1, source_target_pairs={{0,1},{1,0},{2,3},{3,2},{4,5},{5,4},{6,7},{7,6},{8,9},{9,8},{10,11... | collective-permute-start | bytes 393224 | tf_op jit(solution)/shard_map/ppermute | solution.py:377
  1.9 37.8 %collective-permute-start.12 = (bf16[128,4096]{1,0:T(8,128)(2,1)}, bf16[128,4096]{1,0:T(8,128)(2,1)S(1)}, u32[]{:S(2)}, u32[]{:S(2)}) collective-permute-start(bf16[128,4096]{1,0:T(8,128)(2,1)} %bitcast.10), channel_id=1, source_target_pairs={{0,1},{1,0},{2,3},{3,2},{4,5},{5,4},{6,7},{7,6},{8,9},{9,8},{10,11... | collective-permute-start | bytes 3145736 | tf_op jit(solution)/shard_map/ppermute | solution.py:377
  2.0 37.7 %collective-permute-start.13 = (bf16[128,4096]{1,0:T(8,128)(2,1)}, bf16[128,4096]{1,0:T(8,128)(2,1)S(1)}, u32[]{:S(2)}, u32[]{:S(2)}) collective-permute-start(bf16[128,4096]{1,0:T(8,128)(2,1)} %bitcast.12), channel_id=1, source_target_pairs={{0,1},{1,0},{2,3},{3,2},{4,5},{5,4},{6,7},{7,6},{8,9},{9,8},{10,11... | collective-permute-start | bytes 3145736 | tf_op jit(solution)/shard_map/ppermute | solution.py:377
  3.1 2.6 %collective-permute-start.6 = (s32[1,128]{1,0:T(1,128)S(1)}, s32[1,128]{1,0:T(1,128)S(1)}, u32[]{:S(2)}, u32[]{:S(2)}) collective-permute-start(s32[1,128]{1,0:T(1,128)S(1)} %add.32), channel_id=1, source_target_pairs={{0,16},{16,0},{32,48},{48,32},{64,80},{80,64},{96,112},{112,96},{1... | collective-permute-start | bytes 1544 | tf_op jit(solution)/shard_map/ppermute | solution.py:396
  5.6 34.0 %copy-start = (bf16[1,128,4096]{2,1,0:T(8,128)(2,1)S(1)}, bf16[1,128,4096]{2,1,0:T(8,128)(2,1)}, u32[]{:S(2)}) copy-start(bf16[1,128,4096]{2,1,0:T(8,128)(2,1)} %param.6) | copy-start | bytes 3145732
  5.6 34.0 %copy-start.1 = (bf16[1,128,4096]{2,1,0:T(8,128)(2,1)S(1)}, bf16[1,128,4096]{2,1,0:T(8,128)(2,1)}, u32[]{:S(2)}) copy-start(bf16[1,128,4096]{2,1,0:T(8,128)(2,1)} %param.9) | copy-start | bytes 3145732
  5.7 34.0 %copy-start.2 = (s32[1,2048]{1,0:T(1,128)S(1)}, s32[1,2048]{1,0:T(1,128)}, u32[]{:S(2)}) copy-start(s32[1,2048]{1,0:T(1,128)} %docs_ref.1) | copy-start | bytes 24580
  5.7 34.0 %copy-start.3 = (s32[1,128]{1,0:T(1,128)S(1)}, s32[1,128]{1,0:T(1,128)}, u32[]{:S(2)}) copy-start(s32[1,128]{1,0:T(1,128)} %live_own.1) | copy-start | bytes 1540
  5.7 4.0 %collective-permute-start.7 = (s32[1,128]{1,0:T(1,128)S(1)}, s32[1,128]{1,0:T(1,128)S(1)}, u32[]{:S(2)}, u32[]{:S(2)}) collective-permute-start(s32[1,128]{1,0:T(1,128)S(1)} %add.33), channel_id=1, source_target_pairs={{0,32},{16,48},{32,0},{48,16},{64,96},{80,112},{96,64},{112,80},{1... | collective-permute-start | bytes 1544 | tf_op jit(solution)/shard_map/ppermute | solution.py:396
  9.9 8.8 %collective-permute-start.8 = (s32[1,128]{1,0:T(1,128)S(1)}, s32[1,128]{1,0:T(1,128)S(1)}, u32[]{:S(2)}, u32[]{:S(2)}) collective-permute-start(s32[1,128]{1,0:T(1,128)S(1)} %add.34), channel_id=1, source_target_pairs={{0,64},{16,80},{32,96},{48,112},{64,0},{80,16},{96,32},{112,48},{1... | collective-permute-start | bytes 1544 | tf_op jit(solution)/shard_map/ppermute | solution.py:398
  16.0 6.4 %collective-permute-start.4 = (bf16[256,512]{1,0:T(8,128)(2,1)S(1)}, bf16[256,512]{1,0:T(8,128)(2,1)S(1)}, u32[]{:S(2)}, u32[]{:S(2)}) collective-permute-start(bf16[256,512]{1,0:T(8,128)(2,1)S(1)} %pad_maximum_fusion.refs_0_), channel_id=1, source_target_pairs={{0,12},{1,13},{2,14},{3,15},{4,0},{5,1},{6,2},{7,3},{8,4},{9,5},{1... | collective-permute-start | bytes 786440 | tf_op jit(solution)/shard_map/ppermute | solution.py:371
  16.6 5.9 %collective-permute-start.3 = (bf16[256,512]{1,0:T(8,128)(2,1)S(1)}, bf16[256,512]{1,0:T(8,128)(2,1)S(1)}, u32[]{:S(2)}, u32[]{:S(2)}) collective-permute-start(bf16[256,512]{1,0:T(8,128)(2,1)S(1)} %pad_maximum_fusion.refs_0_), channel_id=1, source_target_pairs={{0,4},{1,5},{2,6},{3,7},{4,8},{5,9},{6,10},{7,11},{8,12},{9,13},{1... | collective-permute-start | bytes 786440 | tf_op jit(solution)/shard_map/ppermute | solution.py:368
  18.7 6.7 %collective-permute-start.2 = (bf16[256,512]{1,0:T(8,128)(2,1)S(1)}, bf16[256,512]{1,0:T(8,128)(2,1)S(1)}, u32[]{:S(2)}, u32[]{:S(2)}) collective-permute-start(bf16[256,512]{1,0:T(8,128)(2,1)S(1)} %pad_maximum_fusion.refs_0_), channel_id=1, source_target_pairs={{0,2},{1,3},{2,0},{3,1},{4,6},{5,7},{6,4},{7,5},{8,10},{9,11},{10,... | collective-permute-start | bytes 786440 | tf_op jit(solution)/shard_map/ppermute | solution.py:374
  25.4 6.4 %collective-permute-start.10 = (bf16[256,512]{1,0:T(8,128)(2,1)S(1)}, bf16[256,512]{1,0:T(8,128)(2,1)S(1)}, u32[]{:S(2)}, u32[]{:S(2)}) collective-permute-start(bf16[256,512]{1,0:T(8,128)(2,1)S(1)} %collective-permute-done.2.refs_1_), channel_id=1, source_target_pairs={{0,12},{1,13},{2,14},{3,15},{4,0},{5,1},{6,2},{7,3},{8,4},{9,5},{1... | collective-permute-start | bytes 786440 | tf_op jit(solution)/shard_map/ppermute | solution.py:371
  25.4 6.4 %collective-permute-start.9 = (bf16[256,512]{1,0:T(8,128)(2,1)S(1)}, bf16[256,512]{1,0:T(8,128)(2,1)S(1)}, u32[]{:S(2)}, u32[]{:S(2)}) collective-permute-start(bf16[256,512]{1,0:T(8,128)(2,1)S(1)} %collective-permute-done.2.refs_1_), channel_id=1, source_target_pairs={{0,4},{1,5},{2,6},{3,7},{4,8},{5,9},{6,10},{7,11},{8,12},{9,13},{1... | collective-permute-start | bytes 786440 | tf_op jit(solution)/shard_map/ppermute | solution.py:368
  28.1 6.5 %collective-permute-start.14 = (bf16[256,512]{1,0:T(8,128)(2,1)S(1)}, bf16[256,512]{1,0:T(8,128)(2,1)S(1)}, u32[]{:S(2)}, u32[]{:S(2)}) collective-permute-start(bf16[256,512]{1,0:T(8,128)(2,1)S(1)} %collective-permute-done.3.refs_4_), channel_id=1, source_target_pairs={{0,4},{1,5},{2,6},{3,7},{4,8},{5,9},{6,10},{7,11},{8,12},{9,13},{1... | collective-permute-start | bytes 786440 | tf_op jit(solution)/shard_map/ppermute | solution.py:368
  31.9 7.8 %collective-permute-start.15 = (bf16[256,512]{1,0:T(8,128)(2,1)S(1)}, bf16[256,512]{1,0:T(8,128)(2,1)S(1)}, u32[]{:S(2)}, u32[]{:S(2)}) collective-permute-start(bf16[256,512]{1,0:T(8,128)(2,1)S(1)} %collective-permute-done.10.refs_3_), channel_id=1, source_target_pairs={{0,12},{1,13},{2,14},{3,15},{4,0},{5,1},{6,2},{7,3},{8,4},{9,5},{1... | collective-permute-start | bytes 786440 | tf_op jit(solution)/shard_map/ppermute | solution.py:371
  31.9 2.7 %collective-permute-start.11 = (s32[1,128]{1,0:T(1,128)S(1)}, s32[1,128]{1,0:T(1,128)S(1)}, u32[]{:S(2)}, u32[]{:S(2)}) collective-permute-start(s32[1,128]{1,0:T(1,128)S(1)} %add.35), channel_id=1, source_target_pairs={{0,128},{16,144},{32,160},{48,176},{64,192},{80,208},{96,224},{112... | collective-permute-start | bytes 1544 | tf_op jit(solution)/shard_map/ppermute | solution.py:411
  63.4 25.7 %collective-permute-start.16 = (bf16[256,2048]{1,0:T(8,128)(2,1)S(1)}, bf16[256,2048]{1,0:T(8,128)(2,1)S(1)}, u32[]{:S(2)}, u32[]{:S(2)}) collective-permute-start(bf16[256,2048]{1,0:T(8,128)(2,1)S(1)} %get-tuple-element.38), channel_id=1, source_target_pairs={{0,1},{1,0},{2,3},{3,2},{4,5},{5,4},{6,7},{7,6},{8,9},{9,8},{10,11... | collective-permute-start | bytes 3145736 | tf_op jit(solution)/shard_map/ppermute | solution.py:377
  70.3 9.3 %collective-permute-start.21 = (bf16[528,256]{1,0:T(8,128)(2,1)S(1)}, bf16[528,256]{1,0:T(8,128)(2,1)S(1)}, u32[]{:S(2)}, u32[]{:S(2)}) collective-permute-start(bf16[528,256]{1,0:T(8,128)(2,1)S(1)} %get-tuple-element.47), channel_id=1, source_target_pairs={{0,12},{1,13},{2,14},{3,15},{4,0},{5,1},{6,2},{7,3},{8,4},{9,5},{1... | collective-permute-start | bytes 811016 | tf_op jit(solution)/shard_map/ppermute | solution.py:371
  70.3 9.7 %collective-permute-start.18 = (bf16[528,256]{1,0:T(8,128)(2,1)S(1)}, bf16[528,256]{1,0:T(8,128)(2,1)S(1)}, u32[]{:S(2)}, u32[]{:S(2)}) collective-permute-start(bf16[528,256]{1,0:T(8,128)(2,1)S(1)} %get-tuple-element.43), channel_id=1, source_target_pairs={{0,4},{1,5},{2,6},{3,7},{4,8},{5,9},{6,10},{7,11},{8,12},{9,13},{1... | collective-permute-start | bytes 811016 | tf_op jit(solution)/shard_map/ppermute | solution.py:368
  72.9 11.3 %collective-permute-start.20 = (bf16[528,256]{1,0:T(8,128)(2,1)S(1)}, bf16[528,256]{1,0:T(8,128)(2,1)S(1)}, u32[]{:S(2)}, u32[]{:S(2)}) collective-permute-start(bf16[528,256]{1,0:T(8,128)(2,1)S(1)} %get-tuple-element.45), channel_id=1, source_target_pairs={{0,4},{1,5},{2,6},{3,7},{4,8},{5,9},{6,10},{7,11},{8,12},{9,13},{1... | collective-permute-start | bytes 811016 | tf_op jit(solution)/shard_map/ppermute | solution.py:368
  79.6 8.6 %collective-permute-start.22 = (bf16[528,256]{1,0:T(8,128)(2,1)S(1)}, bf16[528,256]{1,0:T(8,128)(2,1)S(1)}, u32[]{:S(2)}, u32[]{:S(2)}) collective-permute-start(bf16[528,256]{1,0:T(8,128)(2,1)S(1)} %add_convert_fusion.1), channel_id=1, source_target_pairs={{0,12},{1,13},{2,14},{3,15},{4,0},{5,1},{6,2},{7,3},{8,4},{9,5},{1... | collective-permute-start | bytes 811016 | tf_op jit(solution)/shard_map/ppermute | solution.py:371
  79.9 14.1 %collective-permute-start.17 = (bf16[528,256]{1,0:T(8,128)(2,1)S(1)}, bf16[528,256]{1,0:T(8,128)(2,1)S(1)}, u32[]{:S(2)}, u32[]{:S(2)}) collective-permute-start(bf16[528,256]{1,0:T(8,128)(2,1)S(1)} %get-tuple-element.41), channel_id=1, source_target_pairs={{0,12},{1,13},{2,14},{3,15},{4,0},{5,1},{6,2},{7,3},{8,4},{9,5},{1... | collective-permute-start | bytes 811016 | tf_op jit(solution)/shard_map/ppermute | solution.py:371
  80.1 13.9 %collective-permute-start.19 = (bf16[528,256]{1,0:T(8,128)(2,1)S(1)}, bf16[528,256]{1,0:T(8,128)(2,1)S(1)}, u32[]{:S(2)}, u32[]{:S(2)}) collective-permute-start(bf16[528,256]{1,0:T(8,128)(2,1)S(1)} %add_convert_fusion.2), channel_id=1, source_target_pairs={{0,4},{1,5},{2,6},{3,7},{4,8},{5,9},{6,10},{7,11},{8,12},{9,13},{1... | collective-permute-start | bytes 811016 | tf_op jit(solution)/shard_map/ppermute | solution.py:368
  88.3 6.9 %collective-permute-start.23 = (bf16[528,256]{1,0:T(8,128)(2,1)S(1)}, bf16[528,256]{1,0:T(8,128)(2,1)S(1)}, u32[]{:S(2)}, u32[]{:S(2)}) collective-permute-start(bf16[528,256]{1,0:T(8,128)(2,1)S(1)} %add_convert_fusion), channel_id=1, source_target_pairs={{0,2},{1,3},{2,0},{3,1},{4,6},{5,7},{6,4},{7,5},{8,10},{9,11},{10,... | collective-permute-start | bytes 811016 | tf_op jit(solution)/shard_map/ppermute | solution.py:374
  95.5 6.1 %collective-permute-start.24 = (bf16[128,512]{1,0:T(8,128)(2,1)S(1)}, bf16[128,512]{1,0:T(8,128)(2,1)S(1)}, u32[]{:S(2)}, u32[]{:S(2)}) collective-permute-start(bf16[128,512]{1,0:T(8,128)(2,1)S(1)} %get-tuple-element.48), channel_id=1, source_target_pairs={{0,1},{1,0},{2,3},{3,2},{4,5},{5,4},{6,7},{7,6},{8,9},{9,8},{10,11... | collective-permute-start | bytes 393224 | tf_op jit(solution)/shard_map/ppermute | solution.py:377
where the time goes:
time: 103 us; the launch traced here: 102 us
  starting transfers between devices  37.5 us (36%)
  waiting for transfers between devices  34.4 us (33%)
  Pallas kernels  26.4 us (26%)
  other arithmetic  3.1 us (3%)
    ppermute x6, waiting for transfers between devices, to_left(): return lax.ppermute(a, 'ctx', move(-4))  25.9 us
    pallas_call x1, Pallas kernels, attention(): pl.pallas_call(attention_kernel, out_shape=(half_rows, half_rows, both_ro...  23.7 us
    ppermute x7, starting transfers between devices, to_core(): return lax.ppermute(a, 'ctx', swap(1))  13 us
    ppermute x6, starting transfers between devices, to_right(): return lax.ppermute(a, 'ctx', move(4))  10.3 us
    ppermute x1, starting transfers between devices, on_device(): count = count + lax.ppermute(count, 'dp', swap(4))  6.14 us
    ppermute x2, starting transfers between devices, on_device(): count = count + lax.ppermute(count, 'dp', swap(bit))  4.71 us
    ppermute x2, waiting for transfers between devices, to_side(): return lax.ppermute(a, 'ctx', swap(2))  4.18 us
  transfers between devices with their start and end apart: 25, of which 11 were waited for; matrix products, arithmetic and copies ran while one was open for 3% of the time, Pallas kernels for 2%

commit v1 on v0

--- a/solution.py
+++ b/solution.py
@@ -394,8 +394,6 @@
     count = live + live_got
     for bit in (1, 2):
         count = count + lax.ppermute(count, "dp", swap(bit))
-    count, _ = lax.optimization_barrier((count, mine))
-    count = count + lax.ppermute(count, "dp", swap(4))
 
     from_left = to_right(mine)
     from_right = to_left(mine)
@@ -407,6 +405,7 @@
     beside_right = to_left(beside)
     opposite = to_right(from_left)
     beside_opposite = to_left(beside_right)
+    count = count + lax.ppermute(count, "dp", swap(6))
     count, _, _ = lax.optimization_barrier((count, beside_left, beside_right))
     count = count + lax.ppermute(count, "dp", swap(8))
     chunks = (

time: 103 us -> 93.3 us (0.906)
  the two profiles are of different devices: /device:TPU:31 before, /device:TPU:63 now
where the time goes in v1:
time: 93.3 us; the launch traced here: 94.1 us
  starting transfers between devices  33.8 us (36%)
  waiting for transfers between devices  29.8 us (32%)
  Pallas kernels  26.4 us (28%)
  other arithmetic  3.23 us (3%)
    pallas_call x1, Pallas kernels, attention(): pl.pallas_call(attention_kernel, out_shape=(half_rows, half_rows, both_ro...  23.7 us
    ppermute x6, waiting for transfers between devices, to_left(): return lax.ppermute(a, 'ctx', move(-4))  18.7 us
    ppermute x7, starting transfers between devices, to_core(): return lax.ppermute(a, 'ctx', swap(1))  12.2 us
    ppermute x6, starting transfers between devices, to_right(): return lax.ppermute(a, 'ctx', move(4))  10.3 us
    ppermute x2, waiting for transfers between devices, to_side(): return lax.ppermute(a, 'ctx', swap(2))  3.62 us
    ppermute x1, starting transfers between devices, on_device(): count = count + lax.ppermute(count, 'dp', swap(6))  3.3 us
    ppermute x6, waiting for transfers between devices, to_right(): return lax.ppermute(a, 'ctx', move(4))  3.09 us
    ppermute x2, starting transfers between devices, on_device(): count = count + lax.ppermute(count, 'dp', swap(bit))  3.08 us
  transfers between devices with their start and end apart: 25, of which 12 were waited for; matrix products, arithmetic and copies ran while one was open for 3% of the time, Pallas kernels for 2%

profile of v1, /device:TPU:63, one launch (start us, length us, event | category | flops | bytes accessed | tf_op | source)
XLA Modules:
  0.0 94.1 jit_solution(12459780708338899591)
XLA Ops:
  0.6 0.8 collective-permute-start.5
  2.4 0.7 add.32
  3.2 1.1 %slice_select_fusion.2 = (bf16[128,256]{1,0:T(8,128)(2,1)S(1)}, bf16[128,256]{1,0:T(8,128)(2,1)S(1)}) fusion(bf16[128,512]{1,0:T(8,128)(2,1)} %bitcast.18, pred[]{:T(512)S(6)} %eq.4, bf16[128,512]{1,0:T(8,128)(2,1)} %bitcast.16), kind=kLoop, calls=%fused_computation.13 | loop fusion | flops 65536 | bytes 393217 | tf_op jit(solution)/shard_map/jit(_where)/select_n | solution.py:385
  4.3 1.3 %collective-permute-done.6 = s32[1,128]{1,0:T(1,128)S(1)} collective-permute-done((s32[1,128]{1,0:T(1,128)S(1)}, s32[1,128]{1,0:T(1,128)S(1)}, u32[]{:S(2)}, u32[]{:S(2)}) %collective-permute-start.6) | collective-permute-done | bytes 544 | tf_op jit(solution)/shard_map/ppermute | solution.py:396
  5.6 3.0 %collective-permute-start.7 = (s32[1,128]{1,0:T(1,128)S(1)}, s32[1,128]{1,0:T(1,128)S(1)}, u32[]{:S(2)}, u32[]{:S(2)}) collective-permute-start(s32[1,128]{1,0:T(1,128)S(1)} %add.33), channel_id=1, source_target_pairs={{0,32},{16,48},{32,0},{48,16},{64,96},{80,112},{96,64},{112,80},{1... | collective-permute-start | bytes 1544 | tf_op jit(solution)/shard_map/ppermute | solution.py:396
  8.7 0.6 collective-permute-start.4
  9.3 2.1 %collective-permute-start.3 = (bf16[256,512]{1,0:T(8,128)(2,1)S(1)}, bf16[256,512]{1,0:T(8,128)(2,1)S(1)}, u32[]{:S(2)}, u32[]{:S(2)}) collective-permute-start(bf16[256,512]{1,0:T(8,128)(2,1)S(1)} %pad_maximum_fusion.refs_0_), channel_id=1, source_target_pairs={{0,4},{1,5},{2,6},{3,7},{4,8},{5,9},{6,10},{7,11},{8,12},{9,13},{1... | collective-permute-start | bytes 786440 | tf_op jit(solution)/shard_map/ppermute | solution.py:368
  11.5 1.0 %collective-permute-start.2 = (bf16[256,512]{1,0:T(8,128)(2,1)S(1)}, bf16[256,512]{1,0:T(8,128)(2,1)S(1)}, u32[]{:S(2)}, u32[]{:S(2)}) collective-permute-start(bf16[256,512]{1,0:T(8,128)(2,1)S(1)} %pad_maximum_fusion.refs_0_), channel_id=1, source_target_pairs={{0,2},{1,3},{2,0},{3,1},{4,6},{5,7},{6,4},{7,5},{8,10},{9,11},{10,... | collective-permute-start | bytes 786440 | tf_op jit(solution)/shard_map/ppermute | solution.py:374
  12.4 3.7 %collective-permute-done.4.refs_2_ = bf16[256,512]{1,0:T(8,128)(2,1)S(1)} collective-permute-done((bf16[256,512]{1,0:T(8,128)(2,1)S(1)}, bf16[256,512]{1,0:T(8,128)(2,1)S(1)}, u32[]{:S(2)}, u32[]{:S(2)}) %collective-permute-start.4) | collective-permute-done | bytes 262176 | tf_op jit(solution)/shard_map/ppermute | solution.py:371
  16.1 2.4 %collective-permute-done.2.refs_1_ = bf16[256,512]{1,0:T(8,128)(2,1)S(1)} collective-permute-done((bf16[256,512]{1,0:T(8,128)(2,1)S(1)}, bf16[256,512]{1,0:T(8,128)(2,1)S(1)}, u32[]{:S(2)}, u32[]{:S(2)}) %collective-permute-start.2) | collective-permute-done | bytes 262176 | tf_op jit(solution)/shard_map/ppermute | solution.py:374
  18.6 2.7 %collective-permute-start.9 = (bf16[256,512]{1,0:T(8,128)(2,1)S(1)}, bf16[256,512]{1,0:T(8,128)(2,1)S(1)}, u32[]{:S(2)}, u32[]{:S(2)}) collective-permute-start(bf16[256,512]{1,0:T(8,128)(2,1)S(1)} %collective-permute-done.2.refs_1_), channel_id=1, source_target_pairs={{0,4},{1,5},{2,6},{3,7},{4,8},{5,9},{6,10},{7,11},{8,12},{9,13},{1... | collective-permute-start | bytes 786440 | tf_op jit(solution)/shard_map/ppermute | solution.py:368
  21.2 3.3 %collective-permute-start.8 = (s32[1,128]{1,0:T(1,128)S(1)}, s32[1,128]{1,0:T(1,128)S(1)}, u32[]{:S(2)}, u32[]{:S(2)}) collective-permute-start(s32[1,128]{1,0:T(1,128)S(1)} %add.34), channel_id=1, source_target_pairs={{0,96},{16,112},{32,64},{48,80},{64,32},{80,48},{96,0},{112,16},{1... | collective-permute-start | bytes 1544 | tf_op jit(solution)/shard_map/ppermute | solution.py:408
  24.5 1.2 %collective-permute-done.8 = s32[1,128]{1,0:T(1,128)S(1)} collective-permute-done((s32[1,128]{1,0:T(1,128)S(1)}, s32[1,128]{1,0:T(1,128)S(1)}, u32[]{:S(2)}, u32[]{:S(2)}) %collective-permute-start.8) | collective-permute-done | bytes 544 | tf_op jit(solution)/shard_map/ppermute | solution.py:408
  25.7 1.5 %collective-permute-start.15 = (bf16[256,512]{1,0:T(8,128)(2,1)S(1)}, bf16[256,512]{1,0:T(8,128)(2,1)S(1)}, u32[]{:S(2)}, u32[]{:S(2)}) collective-permute-start(bf16[256,512]{1,0:T(8,128)(2,1)S(1)} %collective-permute-done.10.refs_3_), channel_id=1, source_target_pairs={{0,12},{1,13},{2,14},{3,15},{4,0},{5,1},{6,2},{7,3},{8,4},{9,5},{1... | collective-permute-start | bytes 786440 | tf_op jit(solution)/shard_map/ppermute | solution.py:371
  27.2 0.5 collective-permute-start.11
  27.7 1.9 %collective-permute-done.11 = s32[1,128]{1,0:T(1,128)S(1)} collective-permute-done((s32[1,128]{1,0:T(1,128)S(1)}, s32[1,128]{1,0:T(1,128)S(1)}, u32[]{:S(2)}, u32[]{:S(2)}) %collective-permute-start.11) | collective-permute-done | bytes 544 | tf_op jit(solution)/shard_map/ppermute | solution.py:410
  29.6 1.6 %collective-permute-done.14.refs_6_ = bf16[256,512]{1,0:T(8,128)(2,1)S(1)} collective-permute-done((bf16[256,512]{1,0:T(8,128)(2,1)S(1)}, bf16[256,512]{1,0:T(8,128)(2,1)S(1)}, u32[]{:S(2)}, u32[]{:S(2)}) %collective-permute-start.14) | collective-permute-done | bytes 262176 | tf_op jit(solution)/shard_map/ppermute | solution.py:368
  31.2 0.9 collective-permute-done.15.refs_7_
  32.2 23.7 %shard_map.93 = (bf16[128,2048]{1,0:T(8,128)(2,1)S(1)}, bf16[128,2048]{1,0:T(8,128)(2,1)S(1)}, bf16[256,2048]{1,0:T(8,128)(2,1)S(1)}, bf16[528,256]{1,0:T(8,128)...) custom-call(s32[1]{0:T(128)} %bitcast.me_ref, ...), custom_call_target="tpu_custom_call" | custom-call | flops 6000000000 | bytes 8000000 | tf_op jit(solution)/shard_map/pallas_call | solution.py:247
  56.0 6.1 %collective-permute-start.16 = (bf16[256,2048]{1,0:T(8,128)(2,1)S(1)}, bf16[256,2048]{1,0:T(8,128)(2,1)S(1)}, u32[]{:S(2)}, u32[]{:S(2)}) collective-permute-start(bf16[256,2048]{1,0:T(8,128)(2,1)S(1)} %get-tuple-element.36), channel_id=1, source_target_pairs={{0,1},{1,0},{2,3},{3,2},{4,5},{5,4},{6,7},{7,6},{8,9},{9,8},{10,11... | collective-permute-start | bytes 3145736 | tf_op jit(solution)/shard_map/ppermute | solution.py:377
  62.0 2.7 %collective-permute-start.18 = (bf16[528,256]{1,0:T(8,128)(2,1)S(1)}, bf16[528,256]{1,0:T(8,128)(2,1)S(1)}, u32[]{:S(2)}, u32[]{:S(2)}) collective-permute-start(bf16[528,256]{1,0:T(8,128)(2,1)S(1)} %get-tuple-element.41), channel_id=1, source_target_pairs={{0,4},{1,5},{2,6},{3,7},{4,8},{5,9},{6,10},{7,11},{8,12},{9,13},{1... | collective-permute-start | bytes 811016 | tf_op jit(solution)/shard_map/ppermute | solution.py:368
  64.8 6.5 %collective-permute-done.21 = bf16[528,256]{1,0:T(8,128)(2,1)S(1)} collective-permute-done((bf16[528,256]{1,0:T(8,128)(2,1)S(1)}, bf16[528,256]{1,0:T(8,128)(2,1)S(1)}, u32[]{:S(2)}, u32[]{:S(2)}) %collective-permute-start.21) | collective-permute-done | bytes 270368 | tf_op jit(solution)/shard_map/ppermute | solution.py:371
  71.9 2.7 %collective-permute-start.19 = (bf16[528,256]{1,0:T(8,128)(2,1)S(1)}, bf16[528,256]{1,0:T(8,128)(2,1)S(1)}, u32[]{:S(2)}, u32[]{:S(2)}) collective-permute-start(bf16[528,256]{1,0:T(8,128)(2,1)S(1)} %add_convert_fusion.2), channel_id=1, source_target_pairs={{0,4},{1,5},{2,6},{3,7},{4,8},{5,9},{6,10},{7,11},{8,12},{9,13},{1... | collective-permute-start | bytes 811016 | tf_op jit(solution)/shard_map/ppermute | solution.py:368
  74.6 1.4 %collective-permute-done.20 = bf16[528,256]{1,0:T(8,128)(2,1)S(1)} collective-permute-done((bf16[528,256]{1,0:T(8,128)(2,1)S(1)}, bf16[528,256]{1,0:T(8,128)(2,1)S(1)}, u32[]{:S(2)}, u32[]{:S(2)}) %collective-permute-start.20) | collective-permute-done | bytes 270368 | tf_op jit(solution)/shard_map/ppermute | solution.py:368
  76.0 4.0 %collective-permute-done.22 = bf16[528,256]{1,0:T(8,128)(2,1)S(1)} collective-permute-done((bf16[528,256]{1,0:T(8,128)(2,1)S(1)}, bf16[528,256]{1,0:T(8,128)(2,1)S(1)}, u32[]{:S(2)}, u32[]{:S(2)}) %collective-permute-start.22) | collective-permute-done | bytes 270368 | tf_op jit(solution)/shard_map/ppermute | solution.py:371
  80.1 1.0 %collective-permute-start.23 = (bf16[528,256]{1,0:T(8,128)(2,1)S(1)}, bf16[528,256]{1,0:T(8,128)(2,1)S(1)}, u32[]{:S(2)}, u32[]{:S(2)}) collective-permute-start(bf16[528,256]{1,0:T(8,128)(2,1)S(1)} %add_convert_fusion), channel_id=1, source_target_pairs={{0,2},{1,3},{2,0},{3,1},{4,6},{5,7},{6,4},{7,5},{8,10},{9,11},{10,... | collective-permute-start | bytes 811016 | tf_op jit(solution)/shard_map/ppermute | solution.py:374
  81.2 1.1 %maximum_bitcast_fusion = bf16[1,128,4096]{2,1,0:T(8,128)(2,1)} fusion(bf16[128,2048]{1,0:T(8,128)(2,1)S(1)} %get-tuple-element.55, bf16[128,2048]{1,0:T(8,128)(2,1)S(1)} %get-tuple-element.54), kind=kLoop, calls=%fused_computation | loop fusion | flops 2097152 | bytes 2097152 | tf_op jit(solution)/shard_map/broadcast_in_dim | solution.py:458
  82.3 3.5 %collective-permute-done.17.refs_1_ = bf16[528,256]{1,0:T(8,128)(2,1)S(1)} collective-permute-done((bf16[528,256]{1,0:T(8,128)(2,1)S(1)}, bf16[528,256]{1,0:T(8,128)(2,1)S(1)}, u32[]{:S(2)}, u32[]{:S(2)}) %collective-permute-start.17) | collective-permute-done | bytes 270368 | tf_op jit(solution)/shard_map/ppermute | solution.py:371
  85.8 1.2 %collective-permute-done.23.refs_3_ = bf16[528,256]{1,0:T(8,128)(2,1)S(1)} collective-permute-done((bf16[528,256]{1,0:T(8,128)(2,1)S(1)}, bf16[528,256]{1,0:T(8,128)(2,1)S(1)}, u32[]{:S(2)}, u32[]{:S(2)}) %collective-permute-start.23) | collective-permute-done | bytes 270368 | tf_op jit(solution)/shard_map/ppermute | solution.py:374
  87.2 4.4 %collective-permute-start.24 = (bf16[128,512]{1,0:T(8,128)(2,1)S(1)}, bf16[128,512]{1,0:T(8,128)(2,1)S(1)}, u32[]{:S(2)}, u32[]{:S(2)}) collective-permute-start(bf16[128,512]{1,0:T(8,128)(2,1)S(1)} %get-tuple-element.46), channel_id=1, source_target_pairs={{0,1},{1,0},{2,3},{3,2},{4,5},{5,4},{6,7},{7,6},{8,9},{9,8},{10,11... | collective-permute-start | bytes 393224 | tf_op jit(solution)/shard_map/ppermute | solution.py:377
  91.6 1.7 %shard_map.95 = bf16[128,4096]{1,0:T(8,128)(2,1)} custom-call(s32[1]{0:T(128)} %bitcast.me_ref, f32[8,128]{1,0:T(8,128)S(1)} %get-tuple-element.47.ratio, bf16[128,2048]{1,0:T(8,128)(2,1)S(1)} %get-tuple-element.48.own, bf16[256,2048]{1,0:T(8,128)(2,1)S(1)} %collective-permute-done.16.got), custom_call_target="tpu_custom_call" | custom-call | flops 1000000 | bytes 2000000 | tf_op jit(solution)/shard_map/pallas_call | solution.py:321
  93.3 0.7 shard_map.96
  (46 shorter events, 2.3 us)
Async XLA Ops:
  0.6 1.8 %collective-permute-start.5 = (s32[1,128]{1,0:T(1,128)}, s32[1,128]{1,0:T(1,128)S(1)}, u32[]{:S(2)}, u32[]{:S(2)}) collective-permute-start(s32[1,128]{1,0:T(1,128)} %live_own.1), channel_id=1, source_target_pairs={{0,1},{1,0},{2,3},{3,2},{4,5},{5,4},{6,7},{7,6},{8,9},{9,8},{10,11... | collective-permute-start | bytes 1544 | tf_op jit(solution)/shard_map/ppermute | solution.py:377
  1.4 7.2 %collective-permute-start = (bf16[128,512]{1,0:T(8,128)(2,1)}, bf16[128,512]{1,0:T(8,128)(2,1)S(1)}, u32[]{:S(2)}, u32[]{:S(2)}) collective-permute-start(bf16[128,512]{1,0:T(8,128)(2,1)} %bitcast.15), channel_id=1, source_target_pairs={{0,1},{1,0},{2,3},{3,2},{4,5},{5,4},{6,7},{7,6},{8,9},{9,8},{10,11... | collective-permute-start | bytes 393224 | tf_op jit(solution)/shard_map/ppermute | solution.py:377
  1.5 7.1 %collective-permute-start.1 = (bf16[128,512]{1,0:T(8,128)(2,1)}, bf16[128,512]{1,0:T(8,128)(2,1)S(1)}, u32[]{:S(2)}, u32[]{:S(2)}) collective-permute-start(bf16[128,512]{1,0:T(8,128)(2,1)} %bitcast.17), channel_id=1, source_target_pairs={{0,1},{1,0},{2,3},{3,2},{4,5},{5,4},{6,7},{7,6},{8,9},{9,8},{10,11... | collective-permute-start | bytes 393224 | tf_op jit(solution)/shard_map/ppermute | solution.py:377
  1.9 30.3 %collective-permute-start.12 = (bf16[128,4096]{1,0:T(8,128)(2,1)}, bf16[128,4096]{1,0:T(8,128)(2,1)S(1)}, u32[]{:S(2)}, u32[]{:S(2)}) collective-permute-start(bf16[128,4096]{1,0:T(8,128)(2,1)} %bitcast.10), channel_id=1, source_target_pairs={{0,1},{1,0},{2,3},{3,2},{4,5},{5,4},{6,7},{7,6},{8,9},{9,8},{10,11... | collective-permute-start | bytes 3145736 | tf_op jit(solution)/shard_map/ppermute | solution.py:377
  2.0 30.2 %collective-permute-start.13 = (bf16[128,4096]{1,0:T(8,128)(2,1)}, bf16[128,4096]{1,0:T(8,128)(2,1)S(1)}, u32[]{:S(2)}, u32[]{:S(2)}) collective-permute-start(bf16[128,4096]{1,0:T(8,128)(2,1)} %bitcast.12), channel_id=1, source_target_pairs={{0,1},{1,0},{2,3},{3,2},{4,5},{5,4},{6,7},{7,6},{8,9},{9,8},{10,11... | collective-permute-start | bytes 3145736 | tf_op jit(solution)/shard_map/ppermute | solution.py:377
  3.1 29.1 %copy-start = (bf16[1,128,4096]{2,1,0:T(8,128)(2,1)S(1)}, bf16[1,128,4096]{2,1,0:T(8,128)(2,1)}, u32[]{:S(2)}) copy-start(bf16[1,128,4096]{2,1,0:T(8,128)(2,1)} %param.6) | copy-start | bytes 3145732
  3.1 29.1 %copy-start.1 = (bf16[1,128,4096]{2,1,0:T(8,128)(2,1)S(1)}, bf16[1,128,4096]{2,1,0:T(8,128)(2,1)}, u32[]{:S(2)}) copy-start(bf16[1,128,4096]{2,1,0:T(8,128)(2,1)} %param.9) | copy-start | bytes 3145732
  3.1 29.1 %copy-start.2 = (s32[1,2048]{1,0:T(1,128)S(1)}, s32[1,2048]{1,0:T(1,128)}, u32[]{:S(2)}) copy-start(s32[1,2048]{1,0:T(1,128)} %docs_ref.1) | copy-start | bytes 24580
  3.1 29.1 %copy-start.3 = (s32[1,128]{1,0:T(1,128)S(1)}, s32[1,128]{1,0:T(1,128)}, u32[]{:S(2)}) copy-start(s32[1,128]{1,0:T(1,128)} %live_own.1) | copy-start | bytes 1540
  3.1 2.5 %collective-permute-start.6 = (s32[1,128]{1,0:T(1,128)S(1)}, s32[1,128]{1,0:T(1,128)S(1)}, u32[]{:S(2)}, u32[]{:S(2)}) collective-permute-start(s32[1,128]{1,0:T(1,128)S(1)} %add.32), channel_id=1, source_target_pairs={{0,16},{16,0},{32,48},{48,32},{64,80},{80,64},{96,112},{112,96},{1... | collective-permute-start | bytes 1544 | tf_op jit(solution)/shard_map/ppermute | solution.py:396
  5.6 5.9 %collective-permute-start.7 = (s32[1,128]{1,0:T(1,128)S(1)}, s32[1,128]{1,0:T(1,128)S(1)}, u32[]{:S(2)}, u32[]{:S(2)}) collective-permute-start(s32[1,128]{1,0:T(1,128)S(1)} %add.33), channel_id=1, source_target_pairs={{0,32},{16,48},{32,0},{48,16},{64,96},{80,112},{96,64},{112,80},{1... | collective-permute-start | bytes 1544 | tf_op jit(solution)/shard_map/ppermute | solution.py:396
  8.7 7.4 %collective-permute-start.4 = (bf16[256,512]{1,0:T(8,128)(2,1)S(1)}, bf16[256,512]{1,0:T(8,128)(2,1)S(1)}, u32[]{:S(2)}, u32[]{:S(2)}) collective-permute-start(bf16[256,512]{1,0:T(8,128)(2,1)S(1)} %pad_maximum_fusion.refs_0_), channel_id=1, source_target_pairs={{0,12},{1,13},{2,14},{3,15},{4,0},{5,1},{6,2},{7,3},{8,4},{9,5},{1... | collective-permute-start | bytes 786440 | tf_op jit(solution)/shard_map/ppermute | solution.py:371
  9.3 6.8 %collective-permute-start.3 = (bf16[256,512]{1,0:T(8,128)(2,1)S(1)}, bf16[256,512]{1,0:T(8,128)(2,1)S(1)}, u32[]{:S(2)}, u32[]{:S(2)}) collective-permute-start(bf16[256,512]{1,0:T(8,128)(2,1)S(1)} %pad_maximum_fusion.refs_0_), channel_id=1, source_target_pairs={{0,4},{1,5},{2,6},{3,7},{4,8},{5,9},{6,10},{7,11},{8,12},{9,13},{1... | collective-permute-start | bytes 786440 | tf_op jit(solution)/shard_map/ppermute | solution.py:368
  11.5 7.1 %collective-permute-start.2 = (bf16[256,512]{1,0:T(8,128)(2,1)S(1)}, bf16[256,512]{1,0:T(8,128)(2,1)S(1)}, u32[]{:S(2)}, u32[]{:S(2)}) collective-permute-start(bf16[256,512]{1,0:T(8,128)(2,1)S(1)} %pad_maximum_fusion.refs_0_), channel_id=1, source_target_pairs={{0,2},{1,3},{2,0},{3,1},{4,6},{5,7},{6,4},{7,5},{8,10},{9,11},{10,... | collective-permute-start | bytes 786440 | tf_op jit(solution)/shard_map/ppermute | solution.py:374
  18.6 7.2 %collective-permute-start.10 = (bf16[256,512]{1,0:T(8,128)(2,1)S(1)}, bf16[256,512]{1,0:T(8,128)(2,1)S(1)}, u32[]{:S(2)}, u32[]{:S(2)}) collective-permute-start(bf16[256,512]{1,0:T(8,128)(2,1)S(1)} %collective-permute-done.2.refs_1_), channel_id=1, source_target_pairs={{0,12},{1,13},{2,14},{3,15},{4,0},{5,1},{6,2},{7,3},{8,4},{9,5},{1... | collective-permute-start | bytes 786440 | tf_op jit(solution)/shard_map/ppermute | solution.py:371
  18.6 8.7 %collective-permute-start.9 = (bf16[256,512]{1,0:T(8,128)(2,1)S(1)}, bf16[256,512]{1,0:T(8,128)(2,1)S(1)}, u32[]{:S(2)}, u32[]{:S(2)}) collective-permute-start(bf16[256,512]{1,0:T(8,128)(2,1)S(1)} %collective-permute-done.2.refs_1_), channel_id=1, source_target_pairs={{0,4},{1,5},{2,6},{3,7},{4,8},{5,9},{6,10},{7,11},{8,12},{9,13},{1... | collective-permute-start | bytes 786440 | tf_op jit(solution)/shard_map/ppermute | solution.py:368
  21.2 4.5 %collective-permute-start.8 = (s32[1,128]{1,0:T(1,128)S(1)}, s32[1,128]{1,0:T(1,128)S(1)}, u32[]{:S(2)}, u32[]{:S(2)}) collective-permute-start(s32[1,128]{1,0:T(1,128)S(1)} %add.34), channel_id=1, source_target_pairs={{0,96},{16,112},{32,64},{48,80},{64,32},{80,48},{96,0},{112,16},{1... | collective-permute-start | bytes 1544 | tf_op jit(solution)/shard_map/ppermute | solution.py:408
  25.7 5.5 %collective-permute-start.14 = (bf16[256,512]{1,0:T(8,128)(2,1)S(1)}, bf16[256,512]{1,0:T(8,128)(2,1)S(1)}, u32[]{:S(2)}, u32[]{:S(2)}) collective-permute-start(bf16[256,512]{1,0:T(8,128)(2,1)S(1)} %collective-permute-done.3.refs_4_), channel_id=1, source_target_pairs={{0,4},{1,5},{2,6},{3,7},{4,8},{5,9},{6,10},{7,11},{8,12},{9,13},{1... | collective-permute-start | bytes 786440 | tf_op jit(solution)/shard_map/ppermute | solution.py:368
  25.7 6.4 %collective-permute-start.15 = (bf16[256,512]{1,0:T(8,128)(2,1)S(1)}, bf16[256,512]{1,0:T(8,128)(2,1)S(1)}, u32[]{:S(2)}, u32[]{:S(2)}) collective-permute-start(bf16[256,512]{1,0:T(8,128)(2,1)S(1)} %collective-permute-done.10.refs_3_), channel_id=1, source_target_pairs={{0,12},{1,13},{2,14},{3,15},{4,0},{5,1},{6,2},{7,3},{8,4},{9,5},{1... | collective-permute-start | bytes 786440 | tf_op jit(solution)/shard_map/ppermute | solution.py:371
  27.2 2.4 %collective-permute-start.11 = (s32[1,128]{1,0:T(1,128)S(1)}, s32[1,128]{1,0:T(1,128)S(1)}, u32[]{:S(2)}, u32[]{:S(2)}) collective-permute-start(s32[1,128]{1,0:T(1,128)S(1)} %add.35), channel_id=1, source_target_pairs={{0,128},{16,144},{32,160},{48,176},{64,192},{80,208},{96,224},{112... | collective-permute-start | bytes 1544 | tf_op jit(solution)/shard_map/ppermute | solution.py:410
  56.0 25.2 %collective-permute-start.16 = (bf16[256,2048]{1,0:T(8,128)(2,1)S(1)}, bf16[256,2048]{1,0:T(8,128)(2,1)S(1)}, u32[]{:S(2)}, u32[]{:S(2)}) collective-permute-start(bf16[256,2048]{1,0:T(8,128)(2,1)S(1)} %get-tuple-element.36), channel_id=1, source_target_pairs={{0,1},{1,0},{2,3},{3,2},{4,5},{5,4},{6,7},{7,6},{8,9},{9,8},{10,11... | collective-permute-start | bytes 3145736 | tf_op jit(solution)/shard_map/ppermute | solution.py:377
  62.0 9.3 %collective-permute-start.21 = (bf16[528,256]{1,0:T(8,128)(2,1)S(1)}, bf16[528,256]{1,0:T(8,128)(2,1)S(1)}, u32[]{:S(2)}, u32[]{:S(2)}) collective-permute-start(bf16[528,256]{1,0:T(8,128)(2,1)S(1)} %get-tuple-element.45), channel_id=1, source_target_pairs={{0,12},{1,13},{2,14},{3,15},{4,0},{5,1},{6,2},{7,3},{8,4},{9,5},{1... | collective-permute-start | bytes 811016 | tf_op jit(solution)/shard_map/ppermute | solution.py:371
  62.0 9.7 %collective-permute-start.18 = (bf16[528,256]{1,0:T(8,128)(2,1)S(1)}, bf16[528,256]{1,0:T(8,128)(2,1)S(1)}, u32[]{:S(2)}, u32[]{:S(2)}) collective-permute-start(bf16[528,256]{1,0:T(8,128)(2,1)S(1)} %get-tuple-element.41), channel_id=1, source_target_pairs={{0,4},{1,5},{2,6},{3,7},{4,8},{5,9},{6,10},{7,11},{8,12},{9,13},{1... | collective-permute-start | bytes 811016 | tf_op jit(solution)/shard_map/ppermute | solution.py:368
  64.7 11.3 %collective-permute-start.20 = (bf16[528,256]{1,0:T(8,128)(2,1)S(1)}, bf16[528,256]{1,0:T(8,128)(2,1)S(1)}, u32[]{:S(2)}, u32[]{:S(2)}) collective-permute-start(bf16[528,256]{1,0:T(8,128)(2,1)S(1)} %get-tuple-element.43), channel_id=1, source_target_pairs={{0,4},{1,5},{2,6},{3,7},{4,8},{5,9},{6,10},{7,11},{8,12},{9,13},{1... | collective-permute-start | bytes 811016 | tf_op jit(solution)/shard_map/ppermute | solution.py:368
  71.4 8.6 %collective-permute-start.22 = (bf16[528,256]{1,0:T(8,128)(2,1)S(1)}, bf16[528,256]{1,0:T(8,128)(2,1)S(1)}, u32[]{:S(2)}, u32[]{:S(2)}) collective-permute-start(bf16[528,256]{1,0:T(8,128)(2,1)S(1)} %add_convert_fusion.1), channel_id=1, source_target_pairs={{0,12},{1,13},{2,14},{3,15},{4,0},{5,1},{6,2},{7,3},{8,4},{9,5},{1... | collective-permute-start | bytes 811016 | tf_op jit(solution)/shard_map/ppermute | solution.py:371
  71.7 14.1 %collective-permute-start.17 = (bf16[528,256]{1,0:T(8,128)(2,1)S(1)}, bf16[528,256]{1,0:T(8,128)(2,1)S(1)}, u32[]{:S(2)}, u32[]{:S(2)}) collective-permute-start(bf16[528,256]{1,0:T(8,128)(2,1)S(1)} %get-tuple-element.39), channel_id=1, source_target_pairs={{0,12},{1,13},{2,14},{3,15},{4,0},{5,1},{6,2},{7,3},{8,4},{9,5},{1... | collective-permute-start | bytes 811016 | tf_op jit(solution)/shard_map/ppermute | solution.py:371
  71.9 13.9 %collective-permute-start.19 = (bf16[528,256]{1,0:T(8,128)(2,1)S(1)}, bf16[528,256]{1,0:T(8,128)(2,1)S(1)}, u32[]{:S(2)}, u32[]{:S(2)}) collective-permute-start(bf16[528,256]{1,0:T(8,128)(2,1)S(1)} %add_convert_fusion.2), channel_id=1, source_target_pairs={{0,4},{1,5},{2,6},{3,7},{4,8},{5,9},{6,10},{7,11},{8,12},{9,13},{1... | collective-permute-start | bytes 811016 | tf_op jit(solution)/shard_map/ppermute | solution.py:368
  80.1 6.9 %collective-permute-start.23 = (bf16[528,256]{1,0:T(8,128)(2,1)S(1)}, bf16[528,256]{1,0:T(8,128)(2,1)S(1)}, u32[]{:S(2)}, u32[]{:S(2)}) collective-permute-start(bf16[528,256]{1,0:T(8,128)(2,1)S(1)} %add_convert_fusion), channel_id=1, source_target_pairs={{0,2},{1,3},{2,0},{3,1},{4,6},{5,7},{6,4},{7,5},{8,10},{9,11},{10,... | collective-permute-start | bytes 811016 | tf_op jit(solution)/shard_map/ppermute | solution.py:374
  87.2 6.1 %collective-permute-start.24 = (bf16[128,512]{1,0:T(8,128)(2,1)S(1)}, bf16[128,512]{1,0:T(8,128)(2,1)S(1)}, u32[]{:S(2)}, u32[]{:S(2)}) collective-permute-start(bf16[128,512]{1,0:T(8,128)(2,1)S(1)} %get-tuple-element.46), channel_id=1, source_target_pairs={{0,1},{1,0},{2,3},{3,2},{4,5},{5,4},{6,7},{7,6},{8,9},{9,8},{10,11... | collective-permute-start | bytes 393224 | tf_op jit(solution)/shard_map/ppermute | solution.py:377
